TPU v7x, 32 devices: a whole 2x2x4 slice. The times are simulated.
32 devices in a mesh: grp: 8 (over z, core), tp: 4 (over y, x).
Axes of the slice: x: 2, y: 2, z: 4, core: 2. Of those that a mesh axis runs over, the one named last changes fastest.
Arguments:
- query_heads: bfloat16 [4096, 4096], P('grp', 'tp'), may hold values from -6 to 6
- key_heads: bfloat16 [4096, 4096], P('grp', 'tp'), may hold values from -6 to 6
- value_heads: bfloat16 [4096, 4096], P('grp', 'tp'), may hold values from -12 to 12
- modality: int32 [8, 768], P('grp'), may hold values from 0 to 1, as said below
- doc_ids: int32 [8, 768], P('grp'), may hold values from 0 to 188, as said below
- out_weight: bfloat16 [2, 4096, 4096], P(None, 'tp'), may hold values from -0.1875 to 0.1875
- out_grad: bfloat16 [4096, 4096], P('grp'), may hold values from -6 to 6
Outputs:
- layer_output: bfloat16 [4096, 4096], P('grp', 'tp')
- grad_query: bfloat16 [4096, 4096], P('grp', 'tp')
- grad_key: bfloat16 [4096, 4096], P('grp', 'tp')
- grad_value: bfloat16 [4096, 4096], P('grp', 'tp')
Inputs may be any that keep to these rules, and one draw needn't show every extreme that they name: `modality`: row g and row g + 4 describe the same pack. 0 marks a text position, 1 an image position. Positions 0 to 15 alternate text, image. Every pack holds 256 to 512 text positions; some pack holds exactly 512 text positions and some exactly 512 image positions. `doc_ids`: row g and row g + 4 describe the same pack. The document number is 0 at position 0, never falls and rises by at most one a position; a new document starts only at positions of 16 or more that are multiples of 4.
All inputs are finite; a program needn't handle non-finite values.
Results may differ from a plain program's by a relative error of at most 0.028.
Values may be sent and summed in bfloat16 or wider, within the bound.
A program may use at most 128 MiB of HBM per device.

v0:
```python
import jax
import jax.numpy as jnp
from jax import lax
from jax.sharding import PartitionSpec as P

HD = 128


MASKED = -1e30


def from_behind(value, axis, by):
    devices = lax.axis_size(axis)
    return lax.ppermute(value, axis, [(i, (i + by) % devices) for i in range(devices)])


def slot_info(modal_row, doc_row, modal_side, row_count):
    pack_len = modal_row.shape[0]
    chosen = modal_row == modal_side
    slot_pos = jnp.nonzero(chosen, size=row_count, fill_value=pack_len - 1)[0].astype(jnp.int32)
    slot_doc = jnp.take(doc_row, slot_pos)
    live_slot = jnp.arange(row_count, dtype=jnp.int32) < jnp.sum(chosen.astype(jnp.int32))
    return (slot_pos, slot_doc, live_slot)


def allowed(query_info, key_info):
    before = key_info[0][None, :] <= query_info[0][:, None]
    same_doc = key_info[1][None, :] == query_info[1][:, None]
    return before & same_doc & key_info[2][None, :]


def score_block(q_heads, k_heads, permit, factor):
    logits = (
        jnp.einsum("qhd,khd->hqk", q_heads, k_heads, preferred_element_type=jnp.float32) * factor
    )
    return jnp.where(permit[None], logits, MASKED)


def normalizer(score_own, score_cross):
    top_score = jnp.maximum(jnp.max(score_own, axis=2), jnp.max(score_cross, axis=2))
    weight_own = jnp.exp(score_own - top_score[:, :, None])
    weight_cross = jnp.exp(score_cross - top_score[:, :, None])
    denominator = jnp.sum(weight_own, axis=2) + jnp.sum(weight_cross, axis=2)
    return (weight_own, weight_cross, denominator, top_score + jnp.log(denominator))


def row_delta(grad_heads, attended_heads):
    return jnp.transpose(
        jnp.sum(grad_heads.astype(jnp.float32) * attended_heads.astype(jnp.float32), axis=2)
    )


def block_backward(scores, log_total, grad_heads, v_heads, delta_row):
    probability = jnp.exp(scores - log_total[:, :, None])
    grad_prob = jnp.einsum("qhd,khd->hqk", grad_heads, v_heads, preferred_element_type=jnp.float32)
    dscore = (probability * (grad_prob - delta_row[:, :, None])).astype(jnp.bfloat16)
    return (dscore, probability.astype(jnp.bfloat16))


def key_grads(dscore, prob_low, q_heads, grad_heads, factor):
    grad_k = (
        jnp.einsum("hqk,qhd->khd", dscore, q_heads, preferred_element_type=jnp.float32) * factor
    )
    grad_v = jnp.einsum("hqk,qhd->khd", prob_low, grad_heads, preferred_element_type=jnp.float32)
    return (grad_k, grad_v)


def per_device(query_heads, key_heads, value_heads, modality, doc_ids, out_weight, out_grad):
    row_count, col_count = query_heads.shape
    head_count = col_count // HD
    shape3 = (row_count, head_count, HD)
    factor = HD ** (-0.5)
    half_grp = lax.axis_size("grp") // 2
    modal_side = (lax.axis_index("grp") >= half_grp).astype(jnp.int32)
    mine_info = slot_info(modality[0], doc_ids[0], modal_side, row_count)
    peer_info = slot_info(modality[0], doc_ids[0], 1 - modal_side, row_count)
    weight = lax.dynamic_index_in_dim(out_weight, modal_side, 0, keepdims=False)
    q_mine = query_heads.reshape(shape3)
    k_mine = key_heads.reshape(shape3)
    v_mine = value_heads.reshape(shape3)
    arrived = from_behind(jnp.stack((key_heads, value_heads)), "grp", half_grp)
    k_peer = arrived[0].reshape(shape3)
    v_peer = arrived[1].reshape(shape3)
    score_own = score_block(q_mine, k_mine, allowed(mine_info, mine_info), factor)
    score_cross = score_block(q_mine, k_peer, allowed(mine_info, peer_info), factor)
    weight_own, weight_cross, denominator, log_total = normalizer(score_own, score_cross)
    mixed = jnp.einsum(
        "hqk,khd->qhd", weight_own.astype(jnp.bfloat16), v_mine, preferred_element_type=jnp.float32
    )
    mixed = mixed + jnp.einsum(
        "hqk,khd->qhd",
        weight_cross.astype(jnp.bfloat16),
        v_peer,
        preferred_element_type=jnp.float32,
    )
    attended_heads = (mixed / jnp.transpose(denominator)[:, :, None]).astype(jnp.bfloat16)
    attended = attended_heads.reshape(row_count, col_count)
    partial_out = jnp.dot(attended, weight, preferred_element_type=jnp.float32)
    projected = lax.psum_scatter(partial_out, "tp", scatter_dimension=1, tiled=True)
    layer_output = projected.astype(jnp.bfloat16)
    grad_attended = lax.dot_general(
        out_grad, weight, (((1,), (1,)), ((), ())), preferred_element_type=jnp.float32
    ).astype(jnp.bfloat16)
    grad_heads = grad_attended.reshape(shape3)
    delta_row = row_delta(grad_heads, attended_heads)
    dscore_own, prob_own = block_backward(score_own, log_total, grad_heads, v_mine, delta_row)
    dscore_cross, prob_cross = block_backward(score_cross, log_total, grad_heads, v_peer, delta_row)
    grad_q = jnp.einsum("hqk,khd->qhd", dscore_own, k_mine, preferred_element_type=jnp.float32)
    grad_q = (
        grad_q
        + jnp.einsum("hqk,khd->qhd", dscore_cross, k_peer, preferred_element_type=jnp.float32)
    ) * factor
    grad_k_own, grad_v_own = key_grads(dscore_own, prob_own, q_mine, grad_heads, factor)
    grad_k_cross, grad_v_cross = key_grads(dscore_cross, prob_cross, q_mine, grad_heads, factor)
    returned = from_behind(
        jnp.stack((grad_k_cross, grad_v_cross)).astype(jnp.bfloat16), "grp", half_grp
    ).astype(jnp.float32)
    grad_k_add = returned[0]
    grad_v_add = returned[1]
    grad_query = grad_q.astype(jnp.bfloat16).reshape(row_count, col_count)
    grad_key = (grad_k_own + grad_k_add).astype(jnp.bfloat16).reshape(row_count, col_count)
    grad_value = (grad_v_own + grad_v_add).astype(jnp.bfloat16).reshape(row_count, col_count)
    return (layer_output, grad_query, grad_key, grad_value)


def solution(mesh):
    placed = (
        P("grp", "tp"),
        P("grp", "tp"),
        P("grp", "tp"),
        P("grp", None),
        P("grp", None),
        P(None, "tp", None),
        P("grp", None),
    )
    return jax.shard_map(
        per_device,
        mesh=mesh,
        in_specs=placed,
        out_specs=(P("grp", "tp"), P("grp", "tp"), P("grp", "tp"), P("grp", "tp")),
        check_vma=False,
    )
```

profile of v0, /device:TPU:0, one launch (start us, length us, event | category | flops | bytes accessed | tf_op | source)
XLA Modules:
  0.0 264.9 jit_solution(8026931336899967882)
XLA Ops:
  7.2 1.6 copy.80
  8.8 1.5 copy.42
  10.3 1.6 pad_maximum_fusion
  11.9 4.0 %collective-permute-start = (bf16[2,512,1024]{1,2,0:T(8,128)(2,1)}, bf16[2,512,1024]{1,2,0:T(8,128)(2,1)}, u32[]{:S(2)}, u32[]{:S(2)}) collective-permute-start(bf16[2,512,1024]{1,2,0:T(8,128)(2,1)} %pad_maximum_fusion), channel_id=1, source_target_pairs={{0,16},{4,20},{8,24},{12,28},{16,0},{20,4},{24,8},{28,12},{1,17},{... | collective-permute-start | bytes 6291464 | tf_op jit(solution)/shard_map/ppermute | solution.py:14
  16.0 0.6 fusion.83
  16.6 0.3 reduce-window.48
  16.9 0.3 reduce-window.34
  17.3 0.1 slice_reduce_fusion.1
  17.5 5.8 %scatter_custom_fusion = s32[512]{0:T(512)S(1)} fusion(s32[768]{0:T(1024)S(1)} %fusion.74, s32[768]{0:T(1024)S(1)} %broadcast.311, s32[]{:T(128)} %constant.79.clone.1), kind=kCustom, calls=%fused_computation.124 | custom fusion | flops 768 | bytes 2052 | tf_op jit(solution)/shard_map/scatter-add | solution.py:20
  23.4 0.3 reduce-window.36
  23.8 0.1 slice_reduce_fusion.3
  24.0 0.1 slice_reduce_fusion
  24.2 6.0 %scatter_custom_fusion.1 = s32[512]{0:T(512)S(1)} fusion(s32[768]{0:T(1024)S(1)} %fusion.75, s32[768]{0:T(1024)S(1)} %broadcast.311, s32[]{:T(128)} %constant.79.clone.1), kind=kCustom, calls=%fused_computation.122 | custom fusion | flops 768 | bytes 2052 | tf_op jit(solution)/shard_map/scatter-add | solution.py:20
  30.2 0.3 reduce-window.50
  30.7 0.1 slice_reduce_fusion.2
  30.8 1.3 iota_compare_fusion
  32.1 1.4 compare_select_fusion.2
  33.5 2.3 gather_fusion.1
  35.8 2.3 gather_fusion
  38.1 1.4 and_and_fusion
  39.5 1.7 fusion.12
  41.2 0.5 copy-done.12
  41.7 10.2 %fusion.50 = bf16[1024,512]{1,0:T(8,128)(2,1)S(1)} fusion(bf16[512,4096]{1,0:T(8,128)(2,1)S(1)} %copy-done.12, bf16[2,1024,4096]{2,1,0:T(8,128)(2,1)} %param.14, s32[]{:T(128)S(6)} %select_n.94), kind=kOutput, calls=%fused_computation.62 | convolution fusion | flops 4295491584 | bytes 13631492 | tf_op jit(solution)/shard_map/dot_general | solution.py:101
  51.9 54.9 %collective-permute-done = bf16[2,512,1024]{1,2,0:T(8,128)(2,1)} collective-permute-done((bf16[2,512,1024]{1,2,0:T(8,128)(2,1)}, bf16[2,512,1024]{1,2,0:T(8,128)(2,1)}, u32[]{:S(2)}, u32[]{:S(2)}) %collective-permute-start) | collective-permute-done | bytes 2097184 | tf_op jit(solution)/shard_map/ppermute | solution.py:14
  106.8 1.7 fusion.100
  108.5 1.8 fusion.13
  110.3 4.0 %fusion.20 = f32[8,512,128]{1,2,0:T(8,128)} fusion(f32[8,512,512]{1,2,0:T(8,128)S(1)} %get-tuple-element.30, f32[8,512]{1,0:T(8,128)S(1)} %max.10, pred[512,512]{0,1:T(8,128)(4,1)S(1)} %get-tuple-element.28, bf16[512,1024]{1,0:T(8,128)(2,1)S(1)} %copy-done.7), kind=kOutput, calls=%fused_computation.29 | convolution fusion | flops 545259520 | bytes 11812864 | tf_op jit(solution)/shard_map/hqk,khd->qhd/dot_general | solution.py:87
  114.3 3.5 %fusion.6 = (f32[8,512]{1,0:T(8,128)S(1)}, f32[8,512]{1,0:T(8,128)S(1)}) fusion(f32[8,512,512]{2,1,0:T(8,128)S(1)} %get-tuple-element.32, f32[8,512]{1,0:T(8,128)S(1)} %max.10, pred[512,512]{0,1:T(8,128)(4,1)S(1)} %copy-done.5, f32[8,512,512]{1,2,0:T(8,128)S(1)} %get-tuple-element.30, pred[512,512]{0,1:T(8,128)(4,1)S(1)} %get-tuple-element.28), kind=kLoop, calls=%fused_computation.18 | loop fusion | flops 16769024 | bytes 17350656 | tf_op jit(solution)/shard_map/reduce_sum | solution.py:43
  117.9 4.3 %multiply_reduce_fusion = (f32[512,8]{0,1:T(8,128)S(1)}, bf16[512,8,128]{0,2,1:T(8,128)(2,1)S(1)}) fusion(bf16[1024,512]{1,0:T(8,128)(2,1)S(1)} %fusion.50, f32[512,8]{0,1:T(8,128)S(1)} %get-tuple-element.26, bf16[512,8,128]{0,2,1:T(8,128)(2,1)S(1)} %bitcast.191, f32[8,512,512]{2,1,0:T(8,128)S(1)} %get-tuple-element.32, f32[8,512]{1,0:T(8,128)S(1)} %max.10, ...), kind=kOutput, calls=%fused_computation.61 | convolution fusion | flops 548925440 | bytes 13942784 | tf_op jit(solution)/shard_map/hqk,khd->qhd/dot_general | solution.py:90
  122.2 6.9 %fusion.2 = f32[512,4096]{1,0:T(8,128)} fusion(bf16[512,1024]{0,1:T(8,128)(2,1)S(1)} %bitcast.189, bf16[2,1024,4096]{2,1,0:T(8,128)(2,1)S(1)} %bitcast.185, s32[]{:T(128)S(6)} %select_n.94), kind=kOutput, calls=%fused_computation.6 | convolution fusion | flops 4294967296 | bytes 17825796 | tf_op jit(solution)/shard_map/dot_general | solution.py:98
  129.1 7.1 %multiply_convert_fusion = bf16[8,512,512]{1,2,0:T(8,128)(2,1)S(1)} fusion(f32[8,512,512]{2,1,0:T(8,128)} %copy-done.2, f32[8,512]{1,0:T(8,128)S(1)} %bitcast.201, f32[8,512]{1,0:T(8,128)S(1)} %get-tuple-element.25, pred[512,512]{0,1:T(8,128)(4,1)} %get-tuple-element.27, bf16[512,8,128]{0,2,1:T(8,128)(2,1)} %bitcast.197, bf16[512,8,128]{0,2,1:T(8,128)(2,1)} %bitcast.192), kind=kOutput, calls=%fused_computation.9 | convolution fusion | flops 549453824 | bytes 14974976 | tf_op jit(solution)/shard_map/qhd,khd->hqk/dot_general | solution.py:55
  136.3 1.6 fusion.59
  137.9 6.0 %fusion.56 = bf16[1,512,8,128]{1,3,2,0:T(8,128)(2,1)S(1)} fusion(bf16[512,8,128]{0,2,1:T(8,128)(2,1)S(1)} %bitcast.198, f32[8,512,512]{2,1,0:T(8,128)} %copy-done.2, f32[8,512]{1,0:T(8,128)S(1)} %get-tuple-element.25, pred[512,512]{0,1:T(8,128)(4,1)S(1)} %copy-done.6), kind=kOutput, calls=%fused_computation.64 | convolution fusion | flops 545783808 | bytes 10764288 | tf_op jit(solution)/shard_map/hqk,qhd->khd/dot_general | solution.py:64
  143.9 1.5 pad_maximum_fusion.1
  145.4 0.1 collective-permute-start.1
  145.6 3.0 %multiply_convert_fusion.1 = bf16[8,512,512]{1,2,0:T(8,128)(2,1)S(1)} fusion(f32[8,512,512]{1,2,0:T(8,128)S(1)} %bitcast.178, f32[8,512]{1,0:T(8,128)S(1)} %bitcast.202, f32[8,512]{1,0:T(8,128)S(1)} %get-tuple-element.25, pred[512,512]{0,1:T(8,128)(4,1)S(1)} %get-tuple-element.28, bf16[512,8,128]{0,2,1:T(8,128)(2,1)S(1)} %bitcast.199, ...), kind=kOutput, calls=%fused_computation.11 | convolution fusion | flops 549453824 | bytes 14974976 | tf_op jit(solution)/shard_map/qhd,khd->hqk/dot_general | solution.py:55
  148.6 1.9 copy-done.3
  150.5 0.7 fusion.101
  151.2 0.8 fusion.43
  152.0 1.6 copy.63
  153.6 84.9 %collective-permute-done.1 = bf16[2,512,8,128]{1,3,2,0:T(8,128)(2,1)} collective-permute-done((bf16[2,512,8,128]{1,3,2,0:T(8,128)(2,1)}, bf16[2,512,8,128]{1,3,2,0:T(8,128)(2,1)}, u32[]{:S(2)}, u32[]{:S(2)}) %collective-permute-start.1) | collective-permute-done | bytes 2097184 | tf_op jit(solution)/shard_map/ppermute | solution.py:14
  238.5 2.2 convert_element_type.96
  240.7 2.0 copy-done.4
  242.6 3.7 %fusion.41 = bf16[512,8,128]{0,2,1:T(8,128)(2,1)S(1)} fusion(f32[2,512,8,128]{1,3,2,0:T(8,128)S(1)} %convert_element_type.96, bf16[8,512,512]{1,2,0:T(8,128)(2,1)} %copy-done.3, bf16[512,1024]{1,0:T(8,128)(2,1)S(1)} %copy-done), kind=kOutput, calls=%fused_computation.51 | convolution fusion | flops 538443776 | bytes 8388608 | tf_op jit(solution)/shard_map/hqk,qhd->khd/dot_general | solution.py:62
  246.3 1.3 copy.64
  247.7 6.3 %fusion.39 = bf16[512,8,128]{0,2,1:T(8,128)(2,1)S(1)} fusion(f32[2,512,8,128]{1,3,2,0:T(8,128)} %copy-done.4, bf16[512,8,128]{0,2,1:T(8,128)(2,1)S(1)} %bitcast.200, f32[8,512,512]{1,2,0:T(8,128)} %copy-done.1, f32[8,512]{1,0:T(8,128)S(1)} %get-tuple-element.25, pred[512,512]{0,1:T(8,128)(4,1)S(1)} %get-tuple-element.28), kind=kOutput, calls=%fused_computation.48 | convolution fusion | flops 546308096 | bytes 12861440 | tf_op jit(solution)/shard_map/hqk,qhd->khd/dot_general | solution.py:64
  254.0 1.3 copy.65
  255.3 2.7 %convert_element_type.87 = bf16[512,1024]{1,0:T(8,128)(2,1)} convert(f32[512,1024]{1,0:T(8,128)} %reduce-scatter.2.cloned.1.call-done) | non-fusion elementwise | flops 524288 | bytes 3145728 | tf_op jit(solution)/shard_map/convert_element_type | solution.py:100
  (66 shorter events, 0.8 us)
Async XLA Ops:
  7.2 32.3 %copy-start = (bf16[512,1024]{1,0:T(8,128)(2,1)S(1)}, bf16[512,1024]{1,0:T(8,128)(2,1)}, u32[]{:S(2)}) copy-start(bf16[512,1024]{1,0:T(8,128)(2,1)} %param.9) | copy-start | bytes 3145732
  7.2 8.8 %copy-start.10 = (s32[1,768]{1,0:T(1,128)S(1)}, s32[1,768]{1,0:T(1,128)}, u32[]{:S(2)}) copy-start(s32[1,768]{1,0:T(1,128)} %param.13) | copy-start | bytes 9220
  7.2 8.8 %copy-start.11 = (s32[1,768]{1,0:T(1,128)S(1)}, s32[1,768]{1,0:T(1,128)}, u32[]{:S(2)}) copy-start(s32[1,768]{1,0:T(1,128)} %param.12) | copy-start | bytes 9220
  7.2 248.1 %reduce-scatter.2.cloned.1.call-start = ((), (), s32[]{:S(2)}) async-start(), calls=%async_computation.1 | async-start | bytes 10485760 | tf_op jit(solution)/shard_map/reduce_scatter | solution.py:99
  11.9 94.9 %collective-permute-start = (bf16[2,512,1024]{1,2,0:T(8,128)(2,1)}, bf16[2,512,1024]{1,2,0:T(8,128)(2,1)}, u32[]{:S(2)}, u32[]{:S(2)}) collective-permute-start(bf16[2,512,1024]{1,2,0:T(8,128)(2,1)} %pad_maximum_fusion), channel_id=1, source_target_pairs={{0,16},{4,20},{8,24},{12,28},{16,0},{20,4},{24,8},{28,12},{1,17},{... | collective-permute-start | bytes 6291464 | tf_op jit(solution)/shard_map/ppermute | solution.py:14
  39.5 2.2 copy-start.12
  41.7 72.6 %copy-start.1 = (f32[8,512,512]{1,2,0:T(8,128)}, f32[8,512,512]{1,2,0:T(8,128)S(1)}, u32[]{:S(2)}) copy-start(f32[8,512,512]{1,2,0:T(8,128)S(1)} %get-tuple-element.30) | copy-start | bytes 25165828
  41.7 66.9 %copy-start.5 = (pred[512,512]{0,1:T(8,128)(4,1)S(1)}, pred[512,512]{0,1:T(8,128)(4,1)}, u32[]{:S(2)}) copy-start(pred[512,512]{0,1:T(8,128)(4,1)} %get-tuple-element.27) | copy-start | bytes 786436
  51.9 65.9 %copy-start.13 = (bf16[1024,512]{1,0:T(8,128)(2,1)}, bf16[1024,512]{1,0:T(8,128)(2,1)S(1)}, u32[]{:S(2)}) copy-start(bf16[1024,512]{1,0:T(8,128)(2,1)S(1)} %fusion.50) | copy-start | bytes 3145732
  51.9 58.4 %copy-start.7 = (bf16[512,1024]{1,0:T(8,128)(2,1)S(1)}, bf16[512,1024]{1,0:T(8,128)(2,1)}, u32[]{:S(2)}) copy-start(bf16[512,1024]{1,0:T(8,128)(2,1)} %param.11) | copy-start | bytes 3145732
  108.5 9.3 %copy-start.9 = (bf16[1,512,1024]{1,2,0:T(8,128)(2,1)}, bf16[1,512,1024]{1,2,0:T(8,128)(2,1)S(1)}, u32[]{:S(2)}) copy-start(bf16[1,512,1024]{1,2,0:T(8,128)(2,1)S(1)} %get-tuple-element.23) | copy-start | bytes 3145732
  110.3 7.6 %copy-start.2 = (f32[8,512,512]{2,1,0:T(8,128)}, f32[8,512,512]{2,1,0:T(8,128)S(1)}, u32[]{:S(2)}) copy-start(f32[8,512,512]{2,1,0:T(8,128)S(1)} %get-tuple-element.32) | copy-start | bytes 25165828
  114.3 7.9 %slice-start.2 = ((s8[16777216]{0:T(1024)(128)(4,1)}), s8[4194304]{0:T(1024)(128)(4,1)S(1)}, s32[]{:S(2)}) async-start(s8[16777216]{0:T(1024)(128)(4,1)} %bitcast.184), calls=%async_computation.4 | async-start | bytes 8388608
  114.3 7.9 %slice-start.3 = ((s8[16777216]{0:T(1024)(128)(4,1)}), s8[4194304]{0:T(1024)(128)(4,1)S(1)}, s32[]{:S(2)}) async-start(s8[16777216]{0:T(1024)(128)(4,1)} %bitcast.184), calls=%async_computation.5 | async-start | bytes 8388608
  117.8 4.3 %slice-start.4 = ((s8[16777216]{0:T(1024)(128)(4,1)}), s8[4194304]{0:T(1024)(128)(4,1)S(1)}, s32[]{:S(2)}) async-start(s8[16777216]{0:T(1024)(128)(4,1)} %bitcast.184), calls=%async_computation.6 | async-start | bytes 8388608
  117.9 4.3 %slice-start.5 = ((s8[16777216]{0:T(1024)(128)(4,1)}), s8[4194304]{0:T(1024)(128)(4,1)S(1)}, s32[]{:S(2)}) async-start(s8[16777216]{0:T(1024)(128)(4,1)} %bitcast.184), calls=%async_computation.7 | async-start | bytes 8388608
  129.1 8.7 %copy-start.6 = (pred[512,512]{0,1:T(8,128)(4,1)S(1)}, pred[512,512]{0,1:T(8,128)(4,1)}, u32[]{:S(2)}) copy-start(pred[512,512]{0,1:T(8,128)(4,1)} %get-tuple-element.27) | copy-start | bytes 786436
  129.1 8.7 %copy-start.14 = (bf16[1024,512]{1,0:T(8,128)(2,1)S(1)}, bf16[1024,512]{1,0:T(8,128)(2,1)}, u32[]{:S(2)}) copy-start(bf16[1024,512]{1,0:T(8,128)(2,1)} %copy-done.13) | copy-start | bytes 3145732
  136.2 9.3 %slice-start = ((s8[8388608]{0:T(1024)(128)(4,1)}), s8[4194304]{0:T(1024)(128)(4,1)S(1)}, s32[]{:S(2)}) async-start(s8[8388608]{0:T(1024)(128)(4,1)} %bitcast.177), calls=%async_computation.2 | async-start | bytes 8388608
  137.8 7.7 %slice-start.1 = ((s8[8388608]{0:T(1024)(128)(4,1)}), s8[4194304]{0:T(1024)(128)(4,1)S(1)}, s32[]{:S(2)}) async-start(s8[8388608]{0:T(1024)(128)(4,1)} %bitcast.177), calls=%async_computation.3 | async-start | bytes 8388608
  137.9 7.7 %copy-start.8 = (bf16[512,1024]{1,0:T(8,128)(2,1)S(1)}, bf16[512,1024]{1,0:T(8,128)(2,1)}, u32[]{:S(2)}) copy-start(bf16[512,1024]{1,0:T(8,128)(2,1)} %param.11) | copy-start | bytes 3145732
  145.4 93.1 %collective-permute-start.1 = (bf16[2,512,8,128]{1,3,2,0:T(8,128)(2,1)}, bf16[2,512,8,128]{1,3,2,0:T(8,128)(2,1)}, u32[]{:S(2)}, u32[]{:S(2)}) collective-permute-start(bf16[2,512,8,128]{1,3,2,0:T(8,128)(2,1)} %pad_maximum_fusion.1), channel_id=1, source_target_pairs={{0,16},{4,20},{8,24},{12,28},{16,0},{20,4},{24,8},{28,12},{1,17},{... | collective-permute-start | bytes 6291464 | tf_op jit(solution)/shard_map/ppermute | solution.py:14
  148.6 1.9 copy-start.3
  153.6 94.1 %copy-start.15 = (bf16[1024,512]{1,0:T(8,128)(2,1)S(1)}, bf16[1024,512]{1,0:T(8,128)(2,1)}, u32[]{:S(2)}) copy-start(bf16[1024,512]{1,0:T(8,128)(2,1)} %copy-done.13) | copy-start | bytes 3145732
  240.7 2.0 copy-start.4
Sparse Core Ops, SparseCore 0:
  129.2 87.5 reduce-scatter.1
where the time goes:
time: 265 us
  waiting for transfers between devices  140 us (53%)
  matrix products  58 us (22%)
  other arithmetic  29.6 us (11%)
  local copies, waits for them, and re-layouts  18.7 us (7%)
  between operations  14.5 us (5%)
  starting transfers between devices  4.22 us (2%)
    ppermute x2, waiting for transfers between devices, from_behind(): lax.ppermute(value, axis, [(i, (i + by) % devices) for i in range(devices)])  140 us
    dot_general x2, matrix products, key_grads(): jnp.einsum('hqk,qhd->khd', prob_low, grad_heads, preferred_element_type=j...  12.3 us
    scatter-add x2, other arithmetic, slot_info(): jnp.nonzero(chosen, size=row_count, fill_value=pack_len - 1)[0]  11.9 us
    dot_general x1, matrix products, per_device(): lax.dot_general(out_grad, weight, (((1,), (1,)), ((), ())), preferred_ele...  10.2 us
    unnamed x48, local copies, waits for them, and re-layouts  10.1 us
    dot_general x2, matrix products, block_backward(): jnp.einsum('qhd,khd->hqk', grad_heads, v_heads, preferred_element_type=jn...  10.1 us
    dot_general x1, matrix products, per_device(): partial_out = jnp.dot(attended, weight, preferred_element_type=jnp.float32)  6.86 us
  transfers between devices with their start and end apart: 3, of which 2 were waited for; matrix products, arithmetic and copies ran while one was open for 27% of the time, Pallas kernels for 0%

commit v1 on v0

v1 whole, which is shorter than its diff:
```python
import functools

import jax
import jax.numpy as jnp
from jax import lax
from jax.experimental import pallas as pl
from jax.experimental.pallas import tpu as pltpu
from jax.sharding import PartitionSpec as P

HD = 128
MASKED = -1e30
NO_KEY = 1 << 20
LAG = 2

NT = (((1,), (1,)), ((), ()))
TN = (((0,), (0,)), ((), ()))
NN = (((1,), (0,)), ((), ()))


def mul(a, b, dims):
    return lax.dot_general(a, b, dims, preferred_element_type=jnp.float32)


def swap(value, axis, by):
    devices = lax.axis_size(axis)
    return lax.ppermute(value, axis, [(i, (i + by) % devices) for i in range(devices)])


def slot_info(modal_row, doc_row, side, row_count):
    spots = jnp.arange(modal_row.shape[0], dtype=jnp.int32)
    slots = jnp.arange(row_count, dtype=jnp.int32)
    chosen = modal_row == side
    rank = jnp.sum(((spots[None, :] <= spots[:, None]) & chosen[None, :]).astype(jnp.int32), axis=1)
    doc_start = jnp.sum((doc_row[None, :] < doc_row[:, None]).astype(jnp.int32), axis=1)
    before = jnp.sum((rank[None, :] <= slots[:, None]).astype(jnp.int32), axis=1)
    slot_pos = jnp.minimum(before, modal_row.shape[0] - 1)
    slot_start = jnp.sum(jnp.where(spots[None, :] == slot_pos[:, None], doc_start[None, :], 0), axis=1)
    live = jnp.sum(chosen.astype(jnp.int32))
    return slot_pos, slot_start, live, jnp.where(slots < live, slot_pos, NO_KEY)


def step_kernel(plan, *refs):
    rows, low, tile, has_attn, has_next, has_ret, ret_base = plan
    up = rows - low
    refs = list(refs)
    n_ref = refs.pop(0)
    n_mine = n_ref[0]
    if has_attn:
        q_ref, k_ref, v_ref, g_ref, qinfo_ref, kpos_ref = (refs.pop(0) for _ in range(6))
    if has_next:
        kn_ref, vn_ref = refs.pop(0), refs.pop(0)
    msg_ref = refs.pop(0)
    if has_ret:
        own_ref = refs.pop(0)
    aliased = (2 if has_attn else 0) + (2 if has_ret else 0)
    outs = refs[len(refs) - (4 if has_attn else 0) - (2 if has_ret else 0):]
    if has_attn:
        att_ref, dq_ref, acc_ref, send_ref = (outs.pop(0) for _ in range(4))
    row_i = lax.broadcasted_iota(jnp.int32, (up, up), 0)
    col_i = lax.broadcasted_iota(jnp.int32, (up, up), 1)
    if has_ret:
        gk_ref, gv_ref = outs
        n_peer = up - n_mine
        unroll = (col_i == row_i + n_peer).astype(jnp.float32).astype(jnp.bfloat16)
        back_up = mul(unroll, msg_ref[low:rows, :], NN)
        back_low = msg_ref[ret_base:ret_base + low, :].astype(jnp.float32)
        total_low = (own_ref[0:low, :] + back_low).astype(jnp.bfloat16)
        total_up = (own_ref[low:rows, :] + back_up).astype(jnp.bfloat16)
        gk_ref[0:low, :] = total_low[:, :HD]
        gv_ref[0:low, :] = total_low[:, HD:]
        gk_ref[low:rows, :] = total_up[:, :HD]
        gv_ref[low:rows, :] = total_up[:, HD:]
    if not has_attn:
        return
    factor = HD ** (-0.5)
    keys = jnp.concatenate((k_ref[...], msg_ref[0:rows, :HD]), axis=0)
    values = jnp.concatenate((v_ref[...], msg_ref[0:rows, HD:]), axis=0)
    kpos = kpos_ref[...]
    dk = dv = None
    for first in range(0, rows, tile):
        here = slice(first, first + tile)
        q = q_ref[here, :]
        g = g_ref[here, :]
        qpos = qinfo_ref[0:1, here]
        qstart = qinfo_ref[1:2, here]
        permit = (kpos <= qpos) & (kpos >= qstart)
        scores = jnp.where(permit, mul(keys, q, NT) * factor, MASKED)
        top = jnp.max(scores, axis=0, keepdims=True)
        weights = jnp.exp(scores - top)
        inverse = 1.0 / jnp.sum(weights, axis=0, keepdims=True)
        att_t = mul(values, weights.astype(jnp.bfloat16), TN) * inverse
        att = jnp.transpose(att_t).astype(jnp.bfloat16)
        att_ref[here, :] = att
        g_t = jnp.transpose(g.astype(jnp.float32))
        delta = jnp.sum(g_t * att_t.astype(jnp.bfloat16).astype(jnp.float32), axis=0, keepdims=True)
        prob = weights * inverse
        grad_prob = mul(values, g, NT)
        dscore = (prob * (grad_prob - delta)).astype(jnp.bfloat16)
        dq_ref[here, :] = jnp.transpose(mul(keys, dscore, TN) * factor).astype(jnp.bfloat16)
        dk_part = mul(dscore, q, NN)
        dv_part = mul(prob.astype(jnp.bfloat16), g, NN)
        dk = dk_part if dk is None else dk + dk_part
        dv = dv_part if dv is None else dv + dv_part
    dk = dk * factor
    acc_ref[:, :HD] = dk[:rows]
    acc_ref[:, HD:] = dv[:rows]
    there = jnp.concatenate((dk[rows:], dv[rows:]), axis=1).astype(jnp.bfloat16)
    roll = (col_i == row_i - n_mine).astype(jnp.float32).astype(jnp.bfloat16)
    mixed = mul(roll, there[low:], NN)
    if has_next:
        own_next = jnp.concatenate((kn_ref[low:rows, :], vn_ref[low:rows, :]), axis=1)
        slot = lax.broadcasted_iota(jnp.int32, mixed.shape, 0)
        mixed = jnp.where(slot < n_mine, own_next.astype(jnp.float32), mixed)
        send_ref[0:low, :HD] = kn_ref[0:low, :]
        send_ref[0:low, HD:] = vn_ref[0:low, :]
        send_ref[rows:rows + low, :] = there[:low]
    else:
        send_ref[0:low, :] = there[:low]
    send_ref[low:rows, :] = mixed.astype(jnp.bfloat16)


def run_step(s, heads, low, n_mine, q, k, v, g, qinfo, kpos, msg, own, chains):
    rows, cols = q.shape
    has_attn = s < heads
    has_next = s + LAG < heads
    has_ret = s >= LAG
    ret_base = rows if has_attn else 0
    tile = 256 if rows % 256 == 0 else rows
    plan = (rows, low, tile, has_attn, has_next, has_ret, ret_base)

    def head_block(at):
        return pl.BlockSpec((rows, HD), lambda i: (0, at))

    def whole(array):
        return pl.BlockSpec(array.shape, lambda i: (0,) * array.ndim)

    args = [n_mine]
    specs = [pl.BlockSpec(memory_space=pltpu.SMEM)]
    if has_attn:
        args += [q, k, v, g, qinfo, kpos]
        specs += [head_block(s)] * 4 + [whole(qinfo), whole(kpos)]
    if has_next:
        args += [k, v]
        specs += [head_block(s + LAG)] * 2
    args.append(msg)
    specs.append(whole(msg))
    if has_ret:
        args.append(own)
        specs.append(whole(own))
    out_shape, out_specs, names = [], [], []
    full = jax.ShapeDtypeStruct((rows, cols), jnp.bfloat16)

    def chain_out(name, at):
        names.append(name)
        out_shape.append(full)
        out_specs.append(head_block(at))

    if has_attn:
        chain_out("att", s)
        chain_out("dq", s)
        send_rows = rows + low if has_next else rows
        names.extend(("acc", "send"))
        out_shape.append(jax.ShapeDtypeStruct((rows, 2 * HD), jnp.float32))
        out_shape.append(jax.ShapeDtypeStruct((send_rows, 2 * HD), jnp.bfloat16))
        out_specs.append(pl.BlockSpec((rows, 2 * HD), lambda i: (0, 0)))
        out_specs.append(pl.BlockSpec((send_rows, 2 * HD), lambda i: (0, 0)))
    if has_ret:
        chain_out("dk", s - LAG)
        chain_out("dv", s - LAG)
    aliases = {}
    for at, name in enumerate(names):
        if name in chains:
            aliases[len(args)] = at
            args.append(chains[name])
            specs.append(pl.BlockSpec(memory_space=pl.ANY))
    flops = 12 * rows * 2 * rows * HD if has_attn else 2 * rows * rows * HD
    results = pl.pallas_call(
        functools.partial(step_kernel, plan),
        grid=(1,),
        in_specs=specs,
        out_specs=out_specs,
        out_shape=out_shape,
        input_output_aliases=aliases,
        compiler_params=pltpu.CompilerParams(vmem_limit_bytes=48 * 1024 * 1024),
        cost_estimate=pl.CostEstimate(
            flops=flops, bytes_accessed=12 * rows * HD * 2, transcendentals=2 * rows * rows
        ),
        name="step" + str(s),
    )(*args)
    return dict(zip(names, results))


def per_device(query_heads, key_heads, value_heads, modality, doc_ids, out_weight, out_grad):
    rows, cols = query_heads.shape
    heads = cols // HD
    low = modality.shape[1] - rows
    half_grp = lax.axis_size("grp") // 2
    side = (lax.axis_index("grp") >= half_grp).astype(jnp.int32)
    exchange = functools.partial(swap, axis="grp", by=half_grp)

    def head_of(array, h):
        return array[:, h * HD:(h + 1) * HD]

    arrived = {}
    for h in range(min(LAG, heads)):
        pair = jnp.concatenate((head_of(key_heads, h), head_of(value_heads, h)), axis=1)
        arrived[h] = exchange(pair)
    pos, start, live, key_pos = slot_info(modality[0], doc_ids[0], side, rows)
    _, _, _, peer_key_pos = slot_info(modality[0], doc_ids[0], 1 - side, rows)
    qinfo = jnp.stack((pos, start))
    kpos = jnp.concatenate((key_pos, peer_key_pos))[:, None]
    n_mine = (live - low)[None]
    weight = lax.dynamic_index_in_dim(out_weight, side, 0, keepdims=False)
    grad_attended = lax.dot_general(
        out_grad, weight, NT, preferred_element_type=jnp.float32
    ).astype(jnp.bfloat16)
    chains, owns = {}, {}
    for s in range(heads + LAG):
        found = run_step(
            s, heads, low, n_mine, query_heads, key_heads, value_heads, grad_attended,
            qinfo, kpos, arrived.pop(s), owns.pop(s - LAG, None), chains,
        )
        if "send" in found:
            arrived[s + LAG] = exchange(found.pop("send"))
            owns[s] = found.pop("acc")
        chains.update(found)
        if s == heads - 1:
            partial_out = jnp.dot(chains["att"], weight, preferred_element_type=jnp.float32)
            layer_output = lax.psum_scatter(
                partial_out.astype(jnp.bfloat16), "tp", scatter_dimension=1, tiled=True
            )
    return (layer_output, chains["dq"], chains["dk"], chains["dv"])


def solution(mesh):
    placed = (
        P("grp", "tp"),
        P("grp", "tp"),
        P("grp", "tp"),
        P("grp", None),
        P("grp", None),
        P(None, "tp", None),
        P("grp", None),
    )
    return jax.shard_map(
        per_device,
        mesh=mesh,
        in_specs=placed,
        out_specs=(P("grp", "tp"), P("grp", "tp"), P("grp", "tp"), P("grp", "tp")),
        check_vma=False,
    )
```

time: 265 us -> 220 us (0.83)
  Pallas kernels: 0 us -> 41.3 us
  matrix products: 58 us -> 19.6 us
  other arithmetic: 29.6 us -> 7.12 us
  waiting for transfers between devices: 140 us -> 123 us
  local copies, waits for them, and re-layouts: 18.7 us -> 4.76 us
  starting transfers between devices: 4.22 us -> 9.15 us
    ppermute x2 -> x10, waiting for transfers between devices: 140 us -> 90.9 us  [swap(): lax.ppermute(value, axis, [(i, (i + by) % devices) for i in range(devices)])]
    pallas_call x0 -> x10, Pallas kernels: none -> 41.3 us  [run_step(): pl.pallas_call(functools.partial(step_kernel, plan), grid=(1,), in_specs=...]
    dot_general x14 -> x2, matrix products: 58 us -> 19.6 us  [the longest x1 10.2 us: per_device(): lax.dot_general(out_grad, weight, NT, preferred_element_type=jnp.float32)]
    reduce_scatter x1, waiting for transfers between devices: 0.01 us -> 32.1 us  [per_device(): lax.psum_scatter(partial_out.astype(jnp.bfloat16), 'tp', scatter_dimensio...]
    scatter-add x2 -> x0, other arithmetic: 11.9 us -> none  [slot_info(): jnp.nonzero(chosen, size=row_count, fill_value=pack_len - 1)[0]]
    unnamed x48 -> x12, local copies, waits for them, and re-layouts: 10.1 us -> 2.59 us
    ppermute x2 -> x10, starting transfers between devices: 4.18 us -> 9.11 us  [swap(): lax.ppermute(value, axis, [(i, (i + by) % devices) for i in range(devices)])]
    convert_element_type x2 -> x0, other arithmetic: 4.88 us -> none  [the longest x1 2.72 us: per_device(): layer_output = projected.astype(jnp.bfloat16)]
  transfers between devices with their start and end apart: 3 -> 11, of which waited for: 2 -> 10; matrix products, arithmetic and copies ran while one was open for 27% -> 8% of each run, Pallas kernels for 0% -> 17%
where the time goes in v1:
time: 220 us
  waiting for transfers between devices  123 us (56%)
  Pallas kernels  41.3 us (19%)
  matrix products  19.6 us (9%)
  between operations  14.8 us (7%)
  starting transfers between devices  9.15 us (4%)
  other arithmetic  7.12 us (3%)
  local copies, waits for them, and re-layouts  4.76 us (2%)
    ppermute x10, waiting for transfers between devices, swap(): lax.ppermute(value, axis, [(i, (i + by) % devices) for i in range(devices)])  90.9 us
    pallas_call x10, Pallas kernels, run_step(): pl.pallas_call(functools.partial(step_kernel, plan), grid=(1,), in_specs=...  41.3 us
    reduce_scatter x1, waiting for transfers between devices, per_device(): lax.psum_scatter(partial_out.astype(jnp.bfloat16), 'tp', scatter_dimensio...  32.1 us
    dot_general x1, matrix products, per_device(): lax.dot_general(out_grad, weight, NT, preferred_element_type=jnp.float32)  10.2 us
    dot_general x1, matrix products, per_device(): jnp.dot(chains['att'], weight, preferred_element_type=jnp.float32)  9.39 us
    ppermute x10, starting transfers between devices, swap(): lax.ppermute(value, axis, [(i, (i + by) % devices) for i in range(devices)])  9.11 us
  transfers between devices with their start and end apart: 11, of which 10 were waited for; matrix products, arithmetic and copies ran while one was open for 8% of the time, Pallas kernels for 17%

profile of v1, /device:TPU:0, one launch (start us, length us, event | category | flops | bytes accessed | tf_op | source)
XLA Modules:
  0.0 219.7 jit_solution(6006434103555688755)
XLA Ops:
  7.2 0.0 reduce-scatter.2.cloned.1.call-start
  7.2 1.1 fusion.22
  8.4 0.7 pad_maximum_fusion
  9.1 4.0 %collective-permute-start = (bf16[512,256]{1,0:T(8,128)(2,1)}, bf16[512,256]{1,0:T(8,128)(2,1)S(1)}, u32[]{:S(2)}, u32[]{:S(2)}) collective-permute-start(bf16[512,256]{1,0:T(8,128)(2,1)} %pad_maximum_fusion), channel_id=1, source_target_pairs={{0,16},{4,20},{8,24},{12,28},{16,0},{20,4},{24,8},{28,12},{1,17},{... | collective-permute-start | bytes 786440 | tf_op jit(solution)/shard_map/ppermute | solution.py:26
  13.1 0.7 pad_maximum_fusion.1
  13.9 1.4 fusion.18
  15.3 0.7 compare_reduce_fusion
  16.0 0.2 convert_reduce_fusion
  16.2 0.2 convert_reduce_fusion.3
  16.4 0.2 convert_reduce_fusion.2
  16.6 0.2 convert_reduce_fusion.4
  16.8 0.7 reduce.3
  17.5 0.4 convert_reduce_fusion.1
  17.9 0.0 copy-start
  17.9 0.0 copy-start.1
  17.9 0.0 copy-start.2
  17.9 10.2 %fusion.14.refs_4_ = bf16[512,1024]{1,0:T(8,128)(2,1)} fusion(bf16[512,4096]{1,0:T(8,128)(2,1)} %param.13, bf16[2,1024,4096]{2,1,0:T(8,128)(2,1)} %param.12, s32[]{:T(128)S(6)} %select_n.15), kind=kOutput, calls=%fused_computation.20 | convolution fusion | flops 4295491584 | bytes 13631492 | tf_op jit(solution)/shard_map/dot_general | solution.py:214
  28.2 1.3 fusion.19
  29.4 0.4 select_reduce_fusion
  30.4 1.0 copy.57.refs_6_
  31.5 5.1 %collective-permute-done.1.refs_9_ = bf16[512,256]{1,0:T(8,128)(2,1)} collective-permute-done((bf16[512,256]{1,0:T(8,128)(2,1)}, bf16[512,256]{1,0:T(8,128)(2,1)}, u32[]{:S(2)}, u32[]{:S(2)}) %collective-permute-start.1) | collective-permute-done | bytes 262176 | tf_op jit(solution)/shard_map/ppermute | solution.py:26
  36.6 1.0 copy-done.3
  37.7 4.9 %step0.1 = (bf16[512,1024]{1,0:T(8,128)(2,1)S(1)}, bf16[512,1024]{1,0:T(8,128)(2,1)}, f32[512,256]{1,0:T(8,128)S(1)}, bf16[768,256]{1,0:T(8,128)(2,1)S(1)}) custom-call(s32[1]{0:T(128)} %bitcast.refs_0_, bf16[512,1024]{1,0:T(8,128)(2,1)S(1)} %copy-done.2, bf16[512,1024]{1,0:T(8,128)(2,1)S(1)} %copy-done, bf16[512,1024]{1,0:T(8,128)(2,1)S(1)} %copy-done.1, ...), custom_call_target="tpu_custom_call" | custom-call | flops 805306368 | bytes 1572864 | tf_op jit(solution)/shard_map/step0/pallas_call | solution.py:177
  42.5 4.7 %step1.1 = (bf16[512,1024]{1,0:T(8,128)(2,1)S(1)}, bf16[512,1024]{1,0:T(8,128)(2,1)}, f32[512,256]{1,0:T(8,128)S(1)}, bf16[768,256]{1,0:T(8,128)(2,1)S(1)}) custom-call(s32[1]{0:T(128)} %bitcast.refs_0_, bf16[512,1024]{1,0:T(8,128)(2,1)S(1)} %copy-done.2, bf16[512,1024]{1,0:T(8,128)(2,1)S(1)} %copy-done, ...), custom_call_target="tpu_custom_call", output_to_operand_aliasing={{0}: (10, {}), {1}: (11, {})} | custom-call | flops 805306368 | bytes 1572864 | tf_op jit(solution)/shard_map/step1/pallas_call | solution.py:177
  47.3 2.9 %collective-permute-start.2 = (bf16[768,256]{1,0:T(8,128)(2,1)S(1)}, bf16[768,256]{1,0:T(8,128)(2,1)S(1)}, u32[]{:S(2)}, u32[]{:S(2)}) collective-permute-start(bf16[768,256]{1,0:T(8,128)(2,1)S(1)} %get-tuple-element.54), channel_id=1, source_target_pairs={{0,16},{4,20},{8,24},{12,28},{16,0},{20,4},{24,8},{28,12},{1,17},{... | collective-permute-start | bytes 1179656 | tf_op jit(solution)/shard_map/ppermute | solution.py:26
  50.2 22.1 %collective-permute-done.3.refs_9_ = bf16[768,256]{1,0:T(8,128)(2,1)S(1)} collective-permute-done((bf16[768,256]{1,0:T(8,128)(2,1)S(1)}, bf16[768,256]{1,0:T(8,128)(2,1)S(1)}, u32[]{:S(2)}, u32[]{:S(2)}) %collective-permute-start.3) | collective-permute-done | bytes 393248 | tf_op jit(solution)/shard_map/ppermute | solution.py:26
  72.3 5.1 %step2.1 = (bf16[512,1024]{1,0:T(8,128)(2,1)S(1)}, bf16[512,1024]{1,0:T(8,128)(2,1)}, f32[512,256]{1,0:T(8,128)S(1)}, bf16[768,256]{1,0:T(8,128)(2,1)S(1)}, bf16...) custom-call(s32[1]{0:T(128)} %bitcast.refs_0_, ...), custom_call_target="tpu_custom_call", output_to_operand_aliasing={{0}: (11, {}), {1}: (12, {})} | custom-call | flops 805306368 | bytes 1572864 | tf_op jit(solution)/shard_map/step2/pallas_call | solution.py:177
  77.4 11.4 %collective-permute-done.2.refs_9_ = bf16[768,256]{1,0:T(8,128)(2,1)S(1)} collective-permute-done((bf16[768,256]{1,0:T(8,128)(2,1)S(1)}, bf16[768,256]{1,0:T(8,128)(2,1)S(1)}, u32[]{:S(2)}, u32[]{:S(2)}) %collective-permute-start.2) | collective-permute-done | bytes 393248 | tf_op jit(solution)/shard_map/ppermute | solution.py:26
  88.8 4.9 %step3.1 = (bf16[512,1024]{1,0:T(8,128)(2,1)S(1)}, bf16[512,1024]{1,0:T(8,128)(2,1)}, f32[512,256]{1,0:T(8,128)S(1)}, bf16[768,256]{1,0:T(8,128)(2,1)S(1)}, bf16...) custom-call(s32[1]{0:T(128)} %bitcast.refs_0_, ...), custom_call_target="tpu_custom_call", output_to_operand_aliasing={{0}: (11, {}), {1}: (12, {}), {4}: (13, {}), {5}: (14, {})} | custom-call | flops 805306368 | bytes 1572864 | tf_op jit(solution)/shard_map/step3/pallas_call | solution.py:177
  93.8 3.5 %collective-permute-done.5.refs_9_ = bf16[768,256]{1,0:T(8,128)(2,1)S(1)} collective-permute-done((bf16[768,256]{1,0:T(8,128)(2,1)S(1)}, bf16[768,256]{1,0:T(8,128)(2,1)S(1)}, u32[]{:S(2)}, u32[]{:S(2)}) %collective-permute-start.5) | collective-permute-done | bytes 393248 | tf_op jit(solution)/shard_map/ppermute | solution.py:26
  97.3 4.9 %step4.1 = (bf16[512,1024]{1,0:T(8,128)(2,1)S(1)}, bf16[512,1024]{1,0:T(8,128)(2,1)}, f32[512,256]{1,0:T(8,128)S(1)}, bf16[768,256]{1,0:T(8,128)(2,1)S(1)}, bf16...) custom-call(s32[1]{0:T(128)} %bitcast.refs_0_, ...), custom_call_target="tpu_custom_call", output_to_operand_aliasing={{0}: (11, {}), {1}: (12, {}), {4}: (13, {}), {5}: (14, {})} | custom-call | flops 805306368 | bytes 1572864 | tf_op jit(solution)/shard_map/step4/pallas_call | solution.py:177
  102.2 12.9 %collective-permute-done.4.refs_9_ = bf16[768,256]{1,0:T(8,128)(2,1)S(1)} collective-permute-done((bf16[768,256]{1,0:T(8,128)(2,1)S(1)}, bf16[768,256]{1,0:T(8,128)(2,1)S(1)}, u32[]{:S(2)}, u32[]{:S(2)}) %collective-permute-start.4) | collective-permute-done | bytes 393248 | tf_op jit(solution)/shard_map/ppermute | solution.py:26
  115.1 4.9 %step5.1 = (bf16[512,1024]{1,0:T(8,128)(2,1)S(1)}, bf16[512,1024]{1,0:T(8,128)(2,1)}, f32[512,256]{1,0:T(8,128)S(1)}, bf16[768,256]{1,0:T(8,128)(2,1)S(1)}, bf16...) custom-call(s32[1]{0:T(128)} %bitcast.refs_0_, ...), custom_call_target="tpu_custom_call", output_to_operand_aliasing={{0}: (11, {}), {1}: (12, {}), {4}: (13, {}), {5}: (14, {})} | custom-call | flops 805306368 | bytes 1572864 | tf_op jit(solution)/shard_map/step5/pallas_call | solution.py:177
  120.1 11.7 %collective-permute-done.7.refs_7_ = bf16[768,256]{1,0:T(8,128)(2,1)S(1)} collective-permute-done((bf16[768,256]{1,0:T(8,128)(2,1)S(1)}, bf16[768,256]{1,0:T(8,128)(2,1)S(1)}, u32[]{:S(2)}, u32[]{:S(2)}) %collective-permute-start.7) | collective-permute-done | bytes 393248 | tf_op jit(solution)/shard_map/ppermute | solution.py:26
  131.8 5.1 %step6.1 = (bf16[512,1024]{1,0:T(8,128)(2,1)S(1)}, bf16[512,1024]{1,0:T(8,128)(2,1)}, f32[512,256]{1,0:T(8,128)S(1)}, bf16[512,256]{1,0:T(8,128)(2,1)S(1)}, bf16...) custom-call(s32[1]{0:T(128)} %bitcast.refs_0_, ...), custom_call_target="tpu_custom_call", output_to_operand_aliasing={{0}: (9, {}), {1}: (10, {}), {4}: (11, {}), {5}: (12, {})} | custom-call | flops 805306368 | bytes 1572864 | tf_op jit(solution)/shard_map/step6/pallas_call | solution.py:177
  136.9 9.5 %collective-permute-done.6.refs_7_ = bf16[768,256]{1,0:T(8,128)(2,1)S(1)} collective-permute-done((bf16[768,256]{1,0:T(8,128)(2,1)S(1)}, bf16[768,256]{1,0:T(8,128)(2,1)S(1)}, u32[]{:S(2)}, u32[]{:S(2)}) %collective-permute-start.6) | collective-permute-done | bytes 393248 | tf_op jit(solution)/shard_map/ppermute | solution.py:26
  146.4 4.9 %step7.1 = (bf16[512,1024]{1,0:T(8,128)(2,1)S(1)}, bf16[512,1024]{1,0:T(8,128)(2,1)}, f32[512,256]{1,0:T(8,128)S(1)}, bf16[512,256]{1,0:T(8,128)(2,1)S(1)}, bf16...) custom-call(s32[1]{0:T(128)} %bitcast.refs_0_, ...), custom_call_target="tpu_custom_call", output_to_operand_aliasing={{0}: (9, {}), {1}: (10, {}), {4}: (11, {}), {5}: (12, {})} | custom-call | flops 805306368 | bytes 1572864 | tf_op jit(solution)/shard_map/step7/pallas_call | solution.py:177
  151.3 0.7 copy-done.4
  152.0 9.4 %fusion.6 = bf16[512,4096]{1,0:T(8,128)(2,1)} fusion(bf16[512,1024]{1,0:T(8,128)(2,1)S(1)} %get-tuple-element.88, bf16[2,1024,4096]{2,1,0:T(8,128)(2,1)} %param.12, s32[]{:T(128)S(6)} %select_n.15), kind=kOutput, calls=%fused_computation.6 | convolution fusion | flops 4297064448 | bytes 13631492 | tf_op jit(solution)/shard_map/dot_general | solution.py:228
  161.4 0.0 reduce-scatter.2.cloned.1.call-update
  161.4 0.1 collective-permute-start.9
  161.5 0.8 copy-done.5
  162.3 2.1 collective-permute-start.8
  164.4 12.6 %collective-permute-done.9.refs_1_ = bf16[512,256]{1,0:T(8,128)(2,1)S(1)} collective-permute-done((bf16[512,256]{1,0:T(8,128)(2,1)S(1)}, bf16[512,256]{1,0:T(8,128)(2,1)S(1)}, u32[]{:S(2)}, u32[]{:S(2)}) %collective-permute-start.9) | collective-permute-done | bytes 262176 | tf_op jit(solution)/shard_map/ppermute | solution.py:26
  177.0 0.9 step8.1
  177.9 1.9 collective-permute-done.8.refs_1_
  179.8 0.9 step9.1
  180.7 32.1 %reduce-scatter.2.cloned.1.call-done = bf16[512,1024]{1,0:T(8,128)(2,1)} async-done(((bf16[512,4096]{1,0:T(8,128)(2,1)}), bf16[512,1024]{1,0:T(8,128)(2,1)}) %reduce-scatter.2.cloned.1.call-update) | async-done | bytes 1048592 | tf_op jit(solution)/shard_map/reduce_scatter | solution.py:229
  (15 shorter events, 0.0 us)
Async XLA Ops:
  7.2 205.7 %reduce-scatter.2.cloned.1.call-start = ((), (), s32[]{:S(2)}) async-start(), calls=%async_computation.1 | async-start | bytes 5242880 | tf_op jit(solution)/shard_map/reduce_scatter | solution.py:229
  9.1 33.4 %collective-permute-start = (bf16[512,256]{1,0:T(8,128)(2,1)}, bf16[512,256]{1,0:T(8,128)(2,1)S(1)}, u32[]{:S(2)}, u32[]{:S(2)}) collective-permute-start(bf16[512,256]{1,0:T(8,128)(2,1)} %pad_maximum_fusion), channel_id=1, source_target_pairs={{0,16},{4,20},{8,24},{12,28},{16,0},{20,4},{24,8},{28,12},{1,17},{... | collective-permute-start | bytes 786440 | tf_op jit(solution)/shard_map/ppermute | solution.py:26
  13.9 22.7 %collective-permute-start.1 = (bf16[512,256]{1,0:T(8,128)(2,1)}, bf16[512,256]{1,0:T(8,128)(2,1)}, u32[]{:S(2)}, u32[]{:S(2)}) collective-permute-start(bf16[512,256]{1,0:T(8,128)(2,1)} %pad_maximum_fusion.1), channel_id=1, source_target_pairs={{0,16},{4,20},{8,24},{12,28},{16,0},{20,4},{24,8},{28,12},{1,17},{... | collective-permute-start | bytes 786440 | tf_op jit(solution)/shard_map/ppermute | solution.py:26
  17.9 18.7 %copy-start = (bf16[512,1024]{1,0:T(8,128)(2,1)S(1)}, bf16[512,1024]{1,0:T(8,128)(2,1)}, u32[]{:S(2)}) copy-start(bf16[512,1024]{1,0:T(8,128)(2,1)} %refs_2_.15) | copy-start | bytes 3145732
  17.9 18.7 %copy-start.1 = (bf16[512,1024]{1,0:T(8,128)(2,1)S(1)}, bf16[512,1024]{1,0:T(8,128)(2,1)}, u32[]{:S(2)}) copy-start(bf16[512,1024]{1,0:T(8,128)(2,1)} %refs_3_.15) | copy-start | bytes 3145732
  17.9 18.7 %copy-start.2 = (bf16[512,1024]{1,0:T(8,128)(2,1)S(1)}, bf16[512,1024]{1,0:T(8,128)(2,1)}, u32[]{:S(2)}) copy-start(bf16[512,1024]{1,0:T(8,128)(2,1)} %refs_1_.15) | copy-start | bytes 3145732
  36.6 1.0 copy-start.3
  42.5 29.8 %collective-permute-start.3 = (bf16[768,256]{1,0:T(8,128)(2,1)S(1)}, bf16[768,256]{1,0:T(8,128)(2,1)S(1)}, u32[]{:S(2)}, u32[]{:S(2)}) collective-permute-start(bf16[768,256]{1,0:T(8,128)(2,1)S(1)} %get-tuple-element.56), channel_id=1, source_target_pairs={{0,16},{4,20},{8,24},{12,28},{16,0},{20,4},{24,8},{28,12},{1,17},{... | collective-permute-start | bytes 1179656 | tf_op jit(solution)/shard_map/ppermute | solution.py:26
  47.3 41.5 %collective-permute-start.2 = (bf16[768,256]{1,0:T(8,128)(2,1)S(1)}, bf16[768,256]{1,0:T(8,128)(2,1)S(1)}, u32[]{:S(2)}, u32[]{:S(2)}) collective-permute-start(bf16[768,256]{1,0:T(8,128)(2,1)S(1)} %get-tuple-element.54), channel_id=1, source_target_pairs={{0,16},{4,20},{8,24},{12,28},{16,0},{20,4},{24,8},{28,12},{1,17},{... | collective-permute-start | bytes 1179656 | tf_op jit(solution)/shard_map/ppermute | solution.py:26
  77.4 19.8 %collective-permute-start.5 = (bf16[768,256]{1,0:T(8,128)(2,1)S(1)}, bf16[768,256]{1,0:T(8,128)(2,1)S(1)}, u32[]{:S(2)}, u32[]{:S(2)}) collective-permute-start(bf16[768,256]{1,0:T(8,128)(2,1)S(1)} %get-tuple-element.66), channel_id=1, source_target_pairs={{0,16},{4,20},{8,24},{12,28},{16,0},{20,4},{24,8},{28,12},{1,17},{... | collective-permute-start | bytes 1179656 | tf_op jit(solution)/shard_map/ppermute | solution.py:26
  93.8 21.4 %collective-permute-start.4 = (bf16[768,256]{1,0:T(8,128)(2,1)S(1)}, bf16[768,256]{1,0:T(8,128)(2,1)S(1)}, u32[]{:S(2)}, u32[]{:S(2)}) collective-permute-start(bf16[768,256]{1,0:T(8,128)(2,1)S(1)} %get-tuple-element.64), channel_id=1, source_target_pairs={{0,16},{4,20},{8,24},{12,28},{16,0},{20,4},{24,8},{28,12},{1,17},{... | collective-permute-start | bytes 1179656 | tf_op jit(solution)/shard_map/ppermute | solution.py:26
  102.2 29.6 %collective-permute-start.7 = (bf16[768,256]{1,0:T(8,128)(2,1)S(1)}, bf16[768,256]{1,0:T(8,128)(2,1)S(1)}, u32[]{:S(2)}, u32[]{:S(2)}) collective-permute-start(bf16[768,256]{1,0:T(8,128)(2,1)S(1)} %get-tuple-element.78), channel_id=1, source_target_pairs={{0,16},{4,20},{8,24},{12,28},{16,0},{20,4},{24,8},{28,12},{1,17},{... | collective-permute-start | bytes 1179656 | tf_op jit(solution)/shard_map/ppermute | solution.py:26
  120.1 26.3 %collective-permute-start.6 = (bf16[768,256]{1,0:T(8,128)(2,1)S(1)}, bf16[768,256]{1,0:T(8,128)(2,1)S(1)}, u32[]{:S(2)}, u32[]{:S(2)}) collective-permute-start(bf16[768,256]{1,0:T(8,128)(2,1)S(1)} %get-tuple-element.76), channel_id=1, source_target_pairs={{0,16},{4,20},{8,24},{12,28},{16,0},{20,4},{24,8},{28,12},{1,17},{... | collective-permute-start | bytes 1179656 | tf_op jit(solution)/shard_map/ppermute | solution.py:26
  151.3 0.7 copy-start.4
  161.4 0.9 copy-start.5
  161.4 15.6 %collective-permute-start.9 = (bf16[512,256]{1,0:T(8,128)(2,1)S(1)}, bf16[512,256]{1,0:T(8,128)(2,1)S(1)}, u32[]{:S(2)}, u32[]{:S(2)}) collective-permute-start(bf16[512,256]{1,0:T(8,128)(2,1)S(1)} %get-tuple-element.92), channel_id=1, source_target_pairs={{0,16},{4,20},{8,24},{12,28},{16,0},{20,4},{24,8},{28,12},{1,17},{... | collective-permute-start | bytes 786440 | tf_op jit(solution)/shard_map/ppermute | solution.py:26
  162.3 17.5 %collective-permute-start.8 = (bf16[512,256]{1,0:T(8,128)(2,1)S(1)}, bf16[512,256]{1,0:T(8,128)(2,1)S(1)}, u32[]{:S(2)}, u32[]{:S(2)}) collective-permute-start(bf16[512,256]{1,0:T(8,128)(2,1)S(1)} %copy-done.5), channel_id=1, source_target_pairs={{0,16},{4,20},{8,24},{12,28},{16,0},{20,4},{24,8},{28,12},{1,17},{... | collective-permute-start | bytes 786440 | tf_op jit(solution)/shard_map/ppermute | solution.py:26
Sparse Core Ops, SparseCore 0:
  161.5 51.2 reduce-scatter.1
